TPU v7x, 32 devices: a whole 2x2x4 slice. The times are simulated.
32 devices in a mesh: dp: 2 (over x), pipe: 2 (over core), ctx: 8 (over z, y).
Axes of the slice: x: 2, y: 2, z: 4, core: 2. Of those that a mesh axis runs over, the one named last changes fastest.
Arguments:
- section_input: bfloat16 [2, 2, 1024, 2048], P('dp', 'pipe', 'ctx'), may hold values from -6 to 6
- section_positions: int32 [2, 2, 1024], P('dp', 'pipe', 'ctx'), may hold values from 0 to 1023, as said below
- saved_input: bfloat16 [2, 2, 1024, 2048], P('dp', 'pipe', 'ctx'), may hold values from -6 to 6
- saved_positions: int32 [2, 2, 1024], P('dp', 'pipe', 'ctx'), may hold values from 0 to 1023, as said below
- cotangent: bfloat16 [2, 2, 1024, 2048], P('dp', 'pipe', 'ctx'), may hold values from -6 to 6
- norm_gains: float32 [2, 2, 2, 2048], P(None, 'pipe'), may hold values from -2 to 2
- output_gains: float32 [2, 2, 2048], P(None, 'pipe'), may hold values from 0.25 to 2
- plan: int32 [2, 2, 2], P('dp', 'pipe'), may hold values from 0 to 1
Outputs:
- next_input: bfloat16 [2, 2, 1024, 2048], P('dp', 'pipe', 'ctx')
- upstream_grad: bfloat16 [2, 2, 1024, 2048], P('dp', 'pipe', 'ctx')
- gain_grads: float32 [2, 3, 2048], P('pipe')
Inputs may be any that keep to these rules, and one draw needn't show every extreme that they name: `section_positions`: in every sequence the first position is 0 and each later one is either one more than the position before it or 0 (a new document). `saved_positions`: in every sequence the first position is 0 and each later one is either one more than the position before it or 0 (a new document).
All inputs are finite; a program needn't handle non-finite values.
Results may differ from a plain program's by a relative error of at most 0.0075.
Values may be sent and summed in bfloat16 or wider, within the bound.
A program may use at most 64 MiB of HBM per device.

v0:
```python
import jax
import jax.numpy as jnp
from jax import lax
from jax.sharding import PartitionSpec as P

HEADS = 16
HEAD_DIM = 128
FEATURES = 2048
WINDOW = 512
TOK_DEV = 128
EPSILON = 1e-06


def passed_along(value, axis, steps):
    count = lax.axis_size(axis)
    first, last = (max(0, -steps), min(count, count - steps))
    return lax.ppermute(value, axis, [(source, source + steps) for source in range(first, last)])


def shifted(value, axis, steps):
    count = lax.axis_size(axis)
    pairs = [(source, (source + steps) % count) for source in range(count)]
    return lax.ppermute(value, axis, pairs)


def as_bfloat(values):
    narrow = lax.optimization_barrier(values.astype(jnp.bfloat16)).astype(jnp.float32)
    return values + lax.stop_gradient(narrow - values)


def attend(key_rows, key_pos, key_ok, gains, query_count):
    total_rows = key_rows.shape[0]
    first_row = total_rows - query_count
    shaped = key_rows.reshape(total_rows, HEADS, HEAD_DIM)
    normed = shaped * lax.rsqrt(jnp.mean(shaped * shaped, axis=-1, keepdims=True) + EPSILON)
    query_gain = gains[0].reshape(HEADS, HEAD_DIM)
    key_gain = gains[1].reshape(HEADS, HEAD_DIM)
    queries = as_bfloat(normed[first_row:] * query_gain)
    key_vecs = as_bfloat(normed * key_gain)
    scores = jnp.einsum("qhe,khe->hqk", queries, key_vecs) / jnp.sqrt(jnp.float32(HEAD_DIM))
    query_ids = first_row + jnp.arange(query_count, dtype=jnp.int32)
    key_ids = jnp.arange(total_rows, dtype=jnp.int32)
    distance = query_ids[:, None] - key_ids[None, :]
    query_pos = key_pos[first_row:]
    allowed = (
        (distance >= 0)
        & (distance < WINDOW)
        & (query_pos[:, None] - key_pos[None, :] == distance)
        & key_ok[None, :]
    )
    weights = jnp.where(allowed[None], jnp.exp(scores), jnp.float32(0.0))
    probability = as_bfloat(weights / jnp.sum(weights, axis=-1, keepdims=True))
    mixture = jnp.einsum("hqk,khe->qhe", probability, shaped)
    return key_rows[first_row:] + mixture.reshape(query_count, FEATURES) * gains[2]


def pick_gains(norm_gains, output_gains, lap_index):
    pair_gains = lax.dynamic_index_in_dim(norm_gains, lap_index, 0, keepdims=False)[0]
    out_gain = lax.dynamic_index_in_dim(output_gains, lap_index, 0, keepdims=False)[0]
    return jnp.concatenate([pair_gains, out_gain[None]], axis=0)


def local(
    section_input,
    section_positions,
    saved_input,
    saved_positions,
    cotangent,
    norm_gains,
    output_gains,
    plan,
):
    own_rows = section_input[0, 0]
    own_pos = section_positions[0, 0]
    saved_rows = saved_input[0, 0]
    saved_pos = saved_positions[0, 0]
    incoming = cotangent[0, 0]
    shard_rows = own_rows.shape[0]
    piece_len = min(WINDOW, shard_rows)
    piece_count = WINDOW // piece_len
    shard_index = lax.axis_index("ctx")
    pieces = (own_rows, own_pos, saved_rows, saved_pos)
    received = []
    for reach in range(1, piece_count + 1):
        received.append(passed_along((pieces[0], pieces[1], pieces[2], pieces[3]), "ctx", reach))
    ordered = received[::-1]
    ok_parts = [
        jnp.broadcast_to(shard_index >= reach, (piece_len,)) for reach in range(piece_count, 0, -1)
    ]
    key_ok = jnp.concatenate(ok_parts + [jnp.ones((shard_rows,), bool)])
    forward_gains = pick_gains(norm_gains, output_gains, plan[0, 0, 0])
    backward_gains = pick_gains(norm_gains, output_gains, plan[0, 0, 1])
    forward_keys = jnp.concatenate([piece[0] for piece in ordered] + [own_rows], axis=0).astype(
        jnp.float32
    )
    forward_pos = jnp.concatenate([piece[1] for piece in ordered] + [own_pos], axis=0)
    produced = attend(forward_keys, forward_pos, key_ok, forward_gains, shard_rows).astype(
        jnp.bfloat16
    )
    next_input = shifted(produced, "pipe", 1)
    saved_keys = jnp.concatenate([piece[2] for piece in ordered] + [saved_rows], axis=0).astype(
        jnp.float32
    )
    saved_key_pos = jnp.concatenate([piece[3] for piece in ordered] + [saved_pos], axis=0)

    def local_layer(rows, gains):
        return attend(rows, saved_key_pos, key_ok, gains, shard_rows)

    _, pullback = jax.vjp(local_layer, saved_keys, backward_gains)
    key_grads, gain_grads = pullback(incoming.astype(jnp.float32))
    own_grads = key_grads[WINDOW:]
    arriving = jnp.zeros((piece_len, FEATURES), jnp.float32)
    for reach in range(1, piece_count + 1):
        first = (piece_count - reach) * piece_len
        outgoing = key_grads[first : first + piece_len].astype(jnp.bfloat16)
        arriving = arriving + passed_along(outgoing, "ctx", -reach).astype(jnp.float32)
    own_grads = own_grads.at[shard_rows - piece_len :].add(arriving)
    upstream_grad = shifted(own_grads.astype(jnp.bfloat16), "pipe", -1)
    gain_total = lax.psum(gain_grads, ("dp", "ctx"))
    gain_total = gain_total / jnp.float32(TOK_DEV)
    return (next_input[None, None], upstream_grad[None, None], gain_total[None])


def solution(mesh):
    placed = (
        P("dp", "pipe", "ctx", None),
        P("dp", "pipe", "ctx"),
        P("dp", "pipe", "ctx", None),
        P("dp", "pipe", "ctx"),
        P("dp", "pipe", "ctx", None),
        P(None, "pipe", None, None),
        P(None, "pipe", None),
        P("dp", "pipe", None),
    )
    return jax.shard_map(
        local,
        mesh=mesh,
        in_specs=placed,
        out_specs=(
            P("dp", "pipe", "ctx", None),
            P("dp", "pipe", "ctx", None),
            P("pipe", None, None),
        ),
        check_vma=False,
    )
```

profile of v0, /device:TPU:0, one launch (start us, length us, event | category | flops | bytes accessed | tf_op | source)
XLA Modules:
  0.0 320.6 jit_solution(6539457708362573059)
XLA Ops:
  0.6 6.0 %collective-permute-start.13 = (bf16[128,2048]{1,0:T(8,128)(2,1)}, bf16[128,2048]{1,0:T(8,128)(2,1)S(1)}, u32[]{:S(2)}, u32[]{:S(2)}) collective-permute-start(bf16[128,2048]{1,0:T(8,128)(2,1)} %bitcast.86), channel_id=1, source_target_pairs={{0,4},{1,5},{2,6},{3,7},{8,12},{9,13},{10,14},{11,15},{16,20},{17,... | collective-permute-start | bytes 1572872 | tf_op jit(solution)/shard_map/ppermute | solution.py:17
  6.6 4.5 %collective-permute-start.14 = (bf16[128,2048]{1,0:T(8,128)(2,1)}, bf16[128,2048]{1,0:T(8,128)(2,1)S(1)}, u32[]{:S(2)}, u32[]{:S(2)}) collective-permute-start(bf16[128,2048]{1,0:T(8,128)(2,1)} %bitcast.87), channel_id=1, source_target_pairs={{0,3},{1,4},{2,5},{3,6},{4,7},{8,11},{9,12},{10,13},{11,14},{12,15... | collective-permute-start | bytes 1572872 | tf_op jit(solution)/shard_map/ppermute | solution.py:17
  11.1 1.3 collective-permute-start.15
  12.4 3.9 %collective-permute-start.16 = (bf16[128,2048]{1,0:T(8,128)(2,1)}, bf16[128,2048]{1,0:T(8,128)(2,1)}, u32[]{:S(2)}, u32[]{:S(2)}) collective-permute-start(bf16[128,2048]{1,0:T(8,128)(2,1)} %bitcast.89), channel_id=1, source_target_pairs={{0,1},{1,2},{2,3},{3,4},{4,5},{5,6},{6,7},{8,9},{9,10},{10,11},{11... | collective-permute-start | bytes 1572872 | tf_op jit(solution)/shard_map/ppermute | solution.py:17
  17.6 1.3 fusion.62
  21.5 2.0 copy.43
  23.5 1.3 copy.38
  26.1 2.1 copy.34
  32.1 8.5 %collective-permute-done.4 = s32[128]{0:T(128)S(1)} collective-permute-done((s32[128]{0:T(128)}, s32[128]{0:T(128)S(1)}, u32[]{:S(2)}, u32[]{:S(2)}) %collective-permute-start.4) | collective-permute-done | bytes 544 | tf_op jit(solution)/shard_map/ppermute | solution.py:17
  40.6 38.0 %collective-permute-start.5 = (s32[128]{0:T(128)}, s32[128]{0:T(128)S(1)}, u32[]{:S(2)}, u32[]{:S(2)}) collective-permute-start(s32[128]{0:T(128)} %bitcast.117), channel_id=1, source_target_pairs={{0,3},{1,4},{2,5},{3,6},{4,7},{8,11},{9,12},{10,13},{11,14},{12,15... | collective-permute-start | bytes 1544 | tf_op jit(solution)/shard_map/ppermute | solution.py:17
  78.6 1.4 collective-permute-done.5
  81.3 1.4 collective-permute-done.6
  82.7 6.2 %collective-permute-start.7 = (s32[128]{0:T(128)}, s32[128]{0:T(128)S(1)}, u32[]{:S(2)}, u32[]{:S(2)}) collective-permute-start(s32[128]{0:T(128)} %bitcast.119), channel_id=1, source_target_pairs={{0,1},{1,2},{2,3},{3,4},{4,5},{5,6},{6,7},{8,9},{9,10},{10,11},{11... | collective-permute-start | bytes 1544 | tf_op jit(solution)/shard_map/ppermute | solution.py:17
  89.0 1.4 collective-permute-done.7
  90.4 6.8 %collective-permute-start.9 = (s32[128]{0:T(128)}, s32[128]{0:T(128)S(1)}, u32[]{:S(2)}, u32[]{:S(2)}) collective-permute-start(s32[128]{0:T(128)} %bitcast.111), channel_id=1, source_target_pairs={{0,4},{1,5},{2,6},{3,7},{8,12},{9,13},{10,14},{11,15},{16,20},{17,... | collective-permute-start | bytes 1544 | tf_op jit(solution)/shard_map/ppermute | solution.py:17
  98.6 4.1 %collective-permute-start.10 = (s32[128]{0:T(128)}, s32[128]{0:T(128)S(1)}, u32[]{:S(2)}, u32[]{:S(2)}) collective-permute-start(s32[128]{0:T(128)} %bitcast.112), channel_id=1, source_target_pairs={{0,3},{1,4},{2,5},{3,6},{4,7},{8,11},{9,12},{10,13},{11,14},{12,15... | collective-permute-start | bytes 1544 | tf_op jit(solution)/shard_map/ppermute | solution.py:17
  102.8 1.4 collective-permute-done.10
  104.2 3.4 %collective-permute-start.11 = (s32[128]{0:T(128)}, s32[128]{0:T(128)S(1)}, u32[]{:S(2)}, u32[]{:S(2)}) collective-permute-start(s32[128]{0:T(128)} %bitcast.113), channel_id=1, source_target_pairs={{0,2},{1,3},{2,4},{3,5},{4,6},{5,7},{8,10},{9,11},{10,12},{11,13},... | collective-permute-start | bytes 1544 | tf_op jit(solution)/shard_map/ppermute | solution.py:17
  107.6 1.4 collective-permute-done.11
  109.0 4.1 %collective-permute-start.12 = (s32[128]{0:T(128)}, s32[128]{0:T(128)S(1)}, u32[]{:S(2)}, u32[]{:S(2)}) collective-permute-start(s32[128]{0:T(128)} %bitcast.114), channel_id=1, source_target_pairs={{0,1},{1,2},{2,3},{3,4},{4,5},{5,6},{6,7},{8,9},{9,10},{10,11},{11... | collective-permute-start | bytes 1544 | tf_op jit(solution)/shard_map/ppermute | solution.py:17
  113.1 1.4 collective-permute-done.12
  114.5 19.6 %collective-permute-start = (bf16[128,2048]{1,0:T(8,128)(2,1)}, bf16[128,2048]{1,0:T(8,128)(2,1)}, u32[]{:S(2)}, u32[]{:S(2)}) collective-permute-start(bf16[128,2048]{1,0:T(8,128)(2,1)} %bitcast), channel_id=1, source_target_pairs={{0,4},{1,5},{2,6},{3,7},{8,12},{9,13},{10,14},{11,15},{16,20},{17,... | collective-permute-start | bytes 1572872 | tf_op jit(solution)/shard_map/ppermute | solution.py:17
  135.8 2.1 collective-permute-start.1
  138.9 2.1 collective-permute-start.2
  142.0 3.3 %collective-permute-start.3 = (bf16[128,2048]{1,0:T(8,128)(2,1)}, bf16[128,2048]{1,0:T(8,128)(2,1)}, u32[]{:S(2)}, u32[]{:S(2)}) collective-permute-start(bf16[128,2048]{1,0:T(8,128)(2,1)} %bitcast), channel_id=1, source_target_pairs={{0,1},{1,2},{2,3},{3,4},{4,5},{5,6},{6,7},{8,9},{9,10},{10,11},{11... | collective-permute-start | bytes 1572872 | tf_op jit(solution)/shard_map/ppermute | solution.py:17
  149.9 2.0 copy.42
  156.0 2.7 fusion.14
  158.8 4.1 %fusion.59 = (bf16[16,128,640]{2,1,0:T(8,128)(2,1)}, f32[16,128]{1,0:T(8,128)S(1)}, f32[16,128,640]{2,1,0:T(8,128)S(1)}) fusion(f32[16,128]{1,0:T(8,128)S(1)} %get-tuple-element.51, f32[16,128,640]{2,1,0:T(8,128)S(1)} %get-tuple-element.52, pred[128,640]{1,0:T(8,128)(4,1)S(1)} %get-tuple-element.45, f32[16,128]{1,0:T(8,128)S(1)} %multiply_divide_fusion, ...), kind=kOutput, calls=%fused_computation.121 | convolution fusion | flops 345241600 | bytes 16367616 | tf_op jit(solution)/shard_map/transpose(jvp(hqk,khe->qhe))/dot_general | solution.py:53
  162.9 3.4 %multiply_reduce_fusion.1 = (f32[16,128]{1,0:T(8,128)S(1)}, f32[128,16,128]{0,2,1:T(8,128)S(1)}) fusion(f32[640,16,128]{0,2,1:T(8,128)S(1)} %get-tuple-element.29, f32[16,128]{1,0:T(8,128)S(1)} %bitcast.104, bf16[640,16,128]{0,2,1:T(8,128)(2,1)S(1)} %get-tuple-element.30, bf16[640,16,128]{0,2,1:T(8,128)(2,1)S(1)} %constant_dynamic-update-slice_fusion.7, ...), kind=kOutput, calls=%fused_computation.58 | convolution fusion | flops 352057344 | bytes 17989632 | tf_op jit(solution)/shard_map/transpose(jvp(qhe,khe->hqk))/dot_general | solution.py:40
  166.3 3.9 %fusion.6 = (f32[16,128]{1,0:T(8,128)S(1)}, f32[640,16]{0,1:T(8,128)S(1)}, f32[16,640,128]{1,2,0:T(8,128)S(1)}) fusion(bf16[640,16,128]{0,2,1:T(8,128)(2,1)S(1)} %constant_dynamic-update-slice_fusion.7, f32[640,16]{0,1:T(8,128)S(1)} %fusion.54, f32[128,16,128]{0,2,1:T(8,128)S(1)} %get-tuple-element.38, f32[16,128]{1,0:T(8,128)S(1)} %bitcast.100, ...), kind=kOutput, calls=%fused_computation.19 | convolution fusion | flops 354930688 | bytes 21176320 | tf_op jit(solution)/shard_map/transpose(jvp(qhe,khe->hqk))/dot_general | solution.py:40
  170.3 4.0 %fusion.27 = f32[16,128]{1,0:T(8,128)S(1)} fusion(f32[128,16,128]{2,0,1:T(8,128)S(1)} %copy-done.2, bf16[640,16,128]{0,2,1:T(8,128)(2,1)S(1)} %constant_dynamic-update-slice_fusion.7, bf16[16,128,640]{2,1,0:T(8,128)(2,1)} %get-tuple-element.27, f32[16,128,640]{2,1,0:T(8,128)S(1)} %get-tuple-element.52, f32[16,128]{1,0:T(8,128)S(1)} %get-tuple-element.51, ...), kind=kOutput, calls=%fused_computation.50 | convolution fusion | flops 343930880 | bytes 11632640 | tf_op jit(solution)/shard_map/jvp(hqk,khe->qhe)/dot_general | solution.py:53
  174.3 4.9 %add_add_fusion = f32[640,16,128]{0,2,1:T(8,128)} fusion(bf16[640,16,128]{0,2,1:T(8,128)(2,1)S(1)} %constant_dynamic-update-slice_fusion.7, f32[128,16,128]{0,2,1:T(8,128)S(1)} %get-tuple-element.38, f32[16,640,128]{1,2,0:T(8,128)S(1)} %get-tuple-element.54, f32[640,16]{0,1:T(8,128)S(1)} %multiply_multiply_fusion.1, f32[16,128]{1,0:T(8,128)S(1)} %bitcast.101, ...), kind=kOutput, calls=%fused_computation.4 | convolution fusion | flops 354418688 | bytes 22732800 | tf_op jit(solution)/shard_map/transpose(jvp(hqk,khe->qhe))/dot_general | solution.py:53
  179.2 6.0 %copy.48 = f32[640,2048]{1,0:T(8,128)} copy(f32[640,2048]{0,1:T(8,128)} %bitcast.70) | data formatting | bytes 10485760 | tf_op jit(solution)/shard_map/transpose(jvp())/reshape | solution.py:34
  185.1 6.1 %fusion.60 = (bf16[640,2048]{1,0:T(8,128)(2,1)S(1)}, f32[640,2048]{1,0:T(8,128)}) fusion(f32[640,2048]{1,0:T(8,128)} %copy.48, bf16[128,2048]{1,0:T(8,128)(2,1)S(1)} %bitcast.84), kind=kLoop, calls=%fused_computation.122 | loop fusion | flops 3932160 | bytes 13631488 | tf_op jit(solution)/shard_map/convert.8
  191.2 1.4 fusion.61
  192.6 1.4 collective-permute-start.17
  194.1 1.3 collective-permute-start.18
  195.4 2.0 copy.30
  197.4 1.5 collective-permute-start.19
  198.9 2.0 copy.31
  202.2 2.0 copy.32
  207.8 2.0 copy.33
  212.9 2.8 fusion.12
  216.8 3.3 %fusion.2 = f32[16,128,128]{2,1,0:T(8,128)} fusion(bf16[640,16,128]{0,2,1:T(8,128)(2,1)S(1)} %constant_dynamic-update-slice_fusion, bf16[16,128,640]{2,1,0:T(8,128)(2,1)S(1)} %fusion.29, f32[16,128,640]{2,1,0:T(8,128)S(1)} %get-tuple-element.50, f32[16,128]{1,0:T(8,128)S(1)} %get-tuple-element.49, pred[128,640]{1,0:T(8,128)(4,1)S(1)} %get-tuple-element.46), kind=kOutput, calls=%fused_computation.13 | convolution fusion | flops 343408640 | bytes 11624448 | tf_op jit(solution)/shard_map/hqk,khe->qhe/dot_general | solution.py:53
  220.1 1.6 copy.37
  223.0 21.3 %collective-permute-done.20 = bf16[128,2048]{1,0:T(8,128)(2,1)} collective-permute-done((bf16[128,2048]{1,0:T(8,128)(2,1)}, bf16[128,2048]{1,0:T(8,128)(2,1)}, u32[]{:S(2)}, u32[]{:S(2)}) %collective-permute-start.20) | collective-permute-done | bytes 524320 | tf_op jit(solution)/shard_map/ppermute | solution.py:17
  244.3 2.2 fusion.30
  246.6 71.7 %psum.7 = f32[3,2048]{1,0:T(4,128)S(1)} all-reduce(f32[3,2048]{1,0:T(4,128)S(1)} %pad_add_fusion), channel_id=1, replica_groups=mesh['dp'=2,'pipe'=2,'ctx'=8] {'dp','ctx'}, use_global_device_ids=true, to_apply=%region_9.10 | all-reduce | flops 6144 | bytes 49152 | tf_op jit(solution)/shard_map/psum | solution.py:119
  (86 shorter events, 32.7 us)
Async XLA Ops:
  0.6 135.2 %collective-permute-start.13 = (bf16[128,2048]{1,0:T(8,128)(2,1)}, bf16[128,2048]{1,0:T(8,128)(2,1)S(1)}, u32[]{:S(2)}, u32[]{:S(2)}) collective-permute-start(bf16[128,2048]{1,0:T(8,128)(2,1)} %bitcast.86), channel_id=1, source_target_pairs={{0,4},{1,5},{2,6},{3,7},{8,12},{9,13},{10,14},{11,15},{16,20},{17,... | collective-permute-start | bytes 1572872 | tf_op jit(solution)/shard_map/ppermute | solution.py:17
  6.6 132.3 %collective-permute-start.14 = (bf16[128,2048]{1,0:T(8,128)(2,1)}, bf16[128,2048]{1,0:T(8,128)(2,1)S(1)}, u32[]{:S(2)}, u32[]{:S(2)}) collective-permute-start(bf16[128,2048]{1,0:T(8,128)(2,1)} %bitcast.87), channel_id=1, source_target_pairs={{0,3},{1,4},{2,5},{3,6},{4,7},{8,11},{9,12},{10,13},{11,14},{12,15... | collective-permute-start | bytes 1572872 | tf_op jit(solution)/shard_map/ppermute | solution.py:17
  11.1 130.9 %collective-permute-start.15 = (bf16[128,2048]{1,0:T(8,128)(2,1)}, bf16[128,2048]{1,0:T(8,128)(2,1)S(1)}, u32[]{:S(2)}, u32[]{:S(2)}) collective-permute-start(bf16[128,2048]{1,0:T(8,128)(2,1)} %bitcast.88), channel_id=1, source_target_pairs={{0,2},{1,3},{2,4},{3,5},{4,6},{5,7},{8,10},{9,11},{10,12},{11,13},... | collective-permute-start | bytes 1572872 | tf_op jit(solution)/shard_map/ppermute | solution.py:17
  12.4 137.4 %collective-permute-start.16 = (bf16[128,2048]{1,0:T(8,128)(2,1)}, bf16[128,2048]{1,0:T(8,128)(2,1)}, u32[]{:S(2)}, u32[]{:S(2)}) collective-permute-start(bf16[128,2048]{1,0:T(8,128)(2,1)} %bitcast.89), channel_id=1, source_target_pairs={{0,1},{1,2},{2,3},{3,4},{4,5},{5,6},{6,7},{8,9},{9,10},{10,11},{11... | collective-permute-start | bytes 1572872 | tf_op jit(solution)/shard_map/ppermute | solution.py:17
  16.3 24.3 %collective-permute-start.4 = (s32[128]{0:T(128)}, s32[128]{0:T(128)S(1)}, u32[]{:S(2)}, u32[]{:S(2)}) collective-permute-start(s32[128]{0:T(128)} %bitcast.116), channel_id=1, source_target_pairs={{0,4},{1,5},{2,6},{3,7},{8,12},{9,13},{10,14},{11,15},{16,20},{17,... | collective-permute-start | bytes 1544 | tf_op jit(solution)/shard_map/ppermute | solution.py:17
  40.6 39.4 %collective-permute-start.5 = (s32[128]{0:T(128)}, s32[128]{0:T(128)S(1)}, u32[]{:S(2)}, u32[]{:S(2)}) collective-permute-start(s32[128]{0:T(128)} %bitcast.117), channel_id=1, source_target_pairs={{0,3},{1,4},{2,5},{3,6},{4,7},{8,11},{9,12},{10,13},{11,14},{12,15... | collective-permute-start | bytes 1544 | tf_op jit(solution)/shard_map/ppermute | solution.py:17
  80.0 2.7 collective-permute-start.6
  82.7 7.6 %collective-permute-start.7 = (s32[128]{0:T(128)}, s32[128]{0:T(128)S(1)}, u32[]{:S(2)}, u32[]{:S(2)}) collective-permute-start(s32[128]{0:T(128)} %bitcast.119), channel_id=1, source_target_pairs={{0,1},{1,2},{2,3},{3,4},{4,5},{5,6},{6,7},{8,9},{9,10},{10,11},{11... | collective-permute-start | bytes 1544 | tf_op jit(solution)/shard_map/ppermute | solution.py:17
  90.4 8.2 %collective-permute-start.9 = (s32[128]{0:T(128)}, s32[128]{0:T(128)S(1)}, u32[]{:S(2)}, u32[]{:S(2)}) collective-permute-start(s32[128]{0:T(128)} %bitcast.111), channel_id=1, source_target_pairs={{0,4},{1,5},{2,6},{3,7},{8,12},{9,13},{10,14},{11,15},{16,20},{17,... | collective-permute-start | bytes 1544 | tf_op jit(solution)/shard_map/ppermute | solution.py:17
  98.6 5.6 %collective-permute-start.10 = (s32[128]{0:T(128)}, s32[128]{0:T(128)S(1)}, u32[]{:S(2)}, u32[]{:S(2)}) collective-permute-start(s32[128]{0:T(128)} %bitcast.112), channel_id=1, source_target_pairs={{0,3},{1,4},{2,5},{3,6},{4,7},{8,11},{9,12},{10,13},{11,14},{12,15... | collective-permute-start | bytes 1544 | tf_op jit(solution)/shard_map/ppermute | solution.py:17
  104.2 4.8 %collective-permute-start.11 = (s32[128]{0:T(128)}, s32[128]{0:T(128)S(1)}, u32[]{:S(2)}, u32[]{:S(2)}) collective-permute-start(s32[128]{0:T(128)} %bitcast.113), channel_id=1, source_target_pairs={{0,2},{1,3},{2,4},{3,5},{4,6},{5,7},{8,10},{9,11},{10,12},{11,13},... | collective-permute-start | bytes 1544 | tf_op jit(solution)/shard_map/ppermute | solution.py:17
  109.0 5.6 %collective-permute-start.12 = (s32[128]{0:T(128)}, s32[128]{0:T(128)S(1)}, u32[]{:S(2)}, u32[]{:S(2)}) collective-permute-start(s32[128]{0:T(128)} %bitcast.114), channel_id=1, source_target_pairs={{0,1},{1,2},{2,3},{3,4},{4,5},{5,6},{6,7},{8,9},{9,10},{10,11},{11... | collective-permute-start | bytes 1544 | tf_op jit(solution)/shard_map/ppermute | solution.py:17
  114.5 79.5 %collective-permute-start = (bf16[128,2048]{1,0:T(8,128)(2,1)}, bf16[128,2048]{1,0:T(8,128)(2,1)}, u32[]{:S(2)}, u32[]{:S(2)}) collective-permute-start(bf16[128,2048]{1,0:T(8,128)(2,1)} %bitcast), channel_id=1, source_target_pairs={{0,4},{1,5},{2,6},{3,7},{8,12},{9,13},{10,14},{11,15},{16,20},{17,... | collective-permute-start | bytes 1572872 | tf_op jit(solution)/shard_map/ppermute | solution.py:17
  135.8 61.6 %collective-permute-start.1 = (bf16[128,2048]{1,0:T(8,128)(2,1)}, bf16[128,2048]{1,0:T(8,128)(2,1)}, u32[]{:S(2)}, u32[]{:S(2)}) collective-permute-start(bf16[128,2048]{1,0:T(8,128)(2,1)} %bitcast), channel_id=1, source_target_pairs={{0,3},{1,4},{2,5},{3,6},{4,7},{8,11},{9,12},{10,13},{11,14},{12,15... | collective-permute-start | bytes 1572872 | tf_op jit(solution)/shard_map/ppermute | solution.py:17
  138.9 62.1 %collective-permute-start.2 = (bf16[128,2048]{1,0:T(8,128)(2,1)}, bf16[128,2048]{1,0:T(8,128)(2,1)}, u32[]{:S(2)}, u32[]{:S(2)}) collective-permute-start(bf16[128,2048]{1,0:T(8,128)(2,1)} %bitcast), channel_id=1, source_target_pairs={{0,2},{1,3},{2,4},{3,5},{4,6},{5,7},{8,10},{9,11},{10,12},{11,13},... | collective-permute-start | bytes 1572872 | tf_op jit(solution)/shard_map/ppermute | solution.py:17
  142.0 65.8 %collective-permute-start.3 = (bf16[128,2048]{1,0:T(8,128)(2,1)}, bf16[128,2048]{1,0:T(8,128)(2,1)}, u32[]{:S(2)}, u32[]{:S(2)}) collective-permute-start(bf16[128,2048]{1,0:T(8,128)(2,1)} %bitcast), channel_id=1, source_target_pairs={{0,1},{1,2},{2,3},{3,4},{4,5},{5,6},{6,7},{8,9},{9,10},{10,11},{11... | collective-permute-start | bytes 1572872 | tf_op jit(solution)/shard_map/ppermute | solution.py:17
  166.3 3.9 %copy-start.2 = (f32[128,16,128]{2,0,1:T(8,128)S(1)}, f32[128,16,128]{2,0,1:T(8,128)}, u32[]{:S(2)}) copy-start(f32[128,16,128]{2,0,1:T(8,128)} %copy.50) | copy-start | bytes 3145732
  170.3 4.0 %copy-start.3 = (bf16[16,128,640]{2,1,0:T(8,128)(2,1)S(1)}, bf16[16,128,640]{2,1,0:T(8,128)(2,1)}, u32[]{:S(2)}) copy-start(bf16[16,128,640]{2,1,0:T(8,128)(2,1)} %get-tuple-element.27) | copy-start | bytes 7864324
  179.2 6.0 %copy-start.1 = (bf16[1,1,128,2048]{3,2,1,0:T(8,128)(2,1)S(1)}, bf16[1,1,128,2048]{3,2,1,0:T(8,128)(2,1)}, u32[]{:S(2)}) copy-start(bf16[1,1,128,2048]{3,2,1,0:T(8,128)(2,1)} %param.16) | copy-start | bytes 1572868
  192.6 18.4 %copy-start = (bf16[1,1,128,2048]{2,3,1,0:T(8,128)(2,1)S(1)}, bf16[1,1,128,2048]{2,3,1,0:T(8,128)(2,1)}, u32[]{:S(2)}) copy-start(bf16[1,1,128,2048]{2,3,1,0:T(8,128)(2,1)} %copy.34) | copy-start | bytes 1572868
  192.6 30.3 %collective-permute-start.17 = (bf16[128,2048]{1,0:T(8,128)(2,1)}, bf16[128,2048]{1,0:T(8,128)(2,1)}, u32[]{:S(2)}, u32[]{:S(2)}) collective-permute-start(bf16[128,2048]{1,0:T(8,128)(2,1)} %get-tuple-element.33), channel_id=1, source_target_pairs={{1,0},{2,1},{3,2},{4,3},{5,4},{6,5},{7,6},{9,8},{10,9},{11,10},{12... | collective-permute-start | bytes 1572872 | tf_op jit(solution)/shard_map/ppermute | solution.py:17
  194.1 28.9 %collective-permute-start.18 = (bf16[128,2048]{1,0:T(8,128)(2,1)}, bf16[128,2048]{1,0:T(8,128)(2,1)}, u32[]{:S(2)}, u32[]{:S(2)}) collective-permute-start(bf16[128,2048]{1,0:T(8,128)(2,1)} %get-tuple-element.36), channel_id=1, source_target_pairs={{2,0},{3,1},{4,2},{5,3},{6,4},{7,5},{10,8},{11,9},{12,10},{13,11},... | collective-permute-start | bytes 1572872 | tf_op jit(solution)/shard_map/ppermute | solution.py:17
  197.4 25.6 %collective-permute-start.19 = (bf16[128,2048]{1,0:T(8,128)(2,1)}, bf16[128,2048]{1,0:T(8,128)(2,1)}, u32[]{:S(2)}, u32[]{:S(2)}) collective-permute-start(bf16[128,2048]{1,0:T(8,128)(2,1)} %get-tuple-element.35), channel_id=1, source_target_pairs={{3,0},{4,1},{5,2},{6,3},{7,4},{11,8},{12,9},{13,10},{14,11},{15,12... | collective-permute-start | bytes 1572872 | tf_op jit(solution)/shard_map/ppermute | solution.py:17
  201.0 43.3 %collective-permute-start.20 = (bf16[128,2048]{1,0:T(8,128)(2,1)}, bf16[128,2048]{1,0:T(8,128)(2,1)}, u32[]{:S(2)}, u32[]{:S(2)}) collective-permute-start(bf16[128,2048]{1,0:T(8,128)(2,1)} %get-tuple-element.34), channel_id=1, source_target_pairs={{4,0},{5,1},{6,2},{7,3},{12,8},{13,9},{14,10},{15,11},{20,16},{21,... | collective-permute-start | bytes 1572872 | tf_op jit(solution)/shard_map/ppermute | solution.py:17
  222.9 96.1 %collective-permute-start.8 = (bf16[128,2048]{1,0:T(8,128)(2,1)S(1)}, bf16[128,2048]{1,0:T(8,128)(2,1)S(1)}, u32[]{:S(2)}, u32[]{:S(2)}) collective-permute-start(bf16[128,2048]{1,0:T(8,128)(2,1)S(1)} %add_convert_fusion), channel_id=1, source_target_pairs={{0,8},{8,0},{1,9},{9,1},{2,10},{10,2},{3,11},{11,3},{4,12},{12,4},... | collective-permute-start | bytes 1572872 | tf_op jit(solution)/shard_map/ppermute | solution.py:23
  246.5 72.5 %collective-permute-start.21 = (bf16[128,2048]{1,0:T(8,128)(2,1)S(1)}, bf16[128,2048]{1,0:T(8,128)(2,1)S(1)}, u32[]{:S(2)}, u32[]{:S(2)}) collective-permute-start(bf16[128,2048]{1,0:T(8,128)(2,1)S(1)} %fusion.30), channel_id=1, source_target_pairs={{0,8},{8,0},{1,9},{9,1},{2,10},{10,2},{3,11},{11,3},{4,12},{12,4},... | collective-permute-start | bytes 1572872 | tf_op jit(solution)/shard_map/ppermute | solution.py:23
where the time goes:
time: 322 us; the launch traced here: 321 us
  starting transfers between devices  114 us (35%)
  blocking collectives  71.7 us (22%)
  local copies, waits for them, and re-layouts  47 us (15%)
  waiting for transfers between devices  39 us (12%)
  matrix products  29.1 us (9%)
  other arithmetic  15.1 us (5%)
  between operations  5.06 us (2%)
    ppermute x20, starting transfers between devices, passed_along(): lax.ppermute(value, axis, [(source, source + steps) for source in range(f...  113 us
    psum x1, blocking collectives, local(): gain_total = lax.psum(gain_grads, ('dp', 'ctx'))  71.7 us
    ppermute x20, waiting for transfers between devices, passed_along(): lax.ppermute(value, axis, [(source, source + steps) for source in range(f...  39 us
    unnamed x33, local copies, waits for them, and re-layouts  17.3 us
    dot_general x4, matrix products, attend(): mixture = jnp.einsum('hqk,khe->qhe', probability, shaped)  16.3 us
    ppermute x8, local copies, waits for them, and re-layouts, passed_along(): lax.ppermute(value, axis, [(source, source + steps) for source in range(f...  13.2 us
    dot_general x4, matrix products, attend(): jnp.einsum('qhe,khe->hqk', queries, key_vecs)  12.8 us
  transfers between devices with their start and end apart: 22, of which 9 were waited for; matrix products, arithmetic and copies ran while one was open for 28% of the time, Pallas kernels for 0%

commit v1 on v0

--- a/solution.py
+++ b/solution.py
@@ -116,7 +116,8 @@
         arriving = arriving + passed_along(outgoing, "ctx", -reach).astype(jnp.float32)
     own_grads = own_grads.at[shard_rows - piece_len :].add(arriving)
     upstream_grad = shifted(own_grads.astype(jnp.bfloat16), "pipe", -1)
-    gain_total = lax.psum(gain_grads, ("dp", "ctx"))
+    shards = lax.all_gather(gain_grads, ("dp", "ctx"))
+    gain_total = jnp.sum(shards, axis=0)
     gain_total = gain_total / jnp.float32(TOK_DEV)
     return (next_input[None, None], upstream_grad[None, None], gain_total[None])
 

time: 322 us -> 289 us (0.90)
  blocking collectives: 71.7 us -> 38.4 us
    psum x1 -> x0, blocking collectives: 71.7 us -> none  [local(): gain_total = lax.psum(gain_grads, ('dp', 'ctx'))]
    all_gather x0 -> x1, blocking collectives: none -> 38.4 us  [local(): shards = lax.all_gather(gain_grads, ('dp', 'ctx'))]
  transfers between devices with their start and end apart: 22 -> 22, of which waited for: 9 -> 9; matrix products, arithmetic and copies ran while one was open for 28% -> 31% of each run, Pallas kernels for 0% -> 0%
where the time goes in v1:
time: 289 us; the launch traced here: 287 us
  starting transfers between devices  114 us (39%)
  local copies, waits for them, and re-layouts  47 us (16%)
  waiting for transfers between devices  38.9 us (13%)
  blocking collectives  38.4 us (13%)
  matrix products  29.1 us (10%)
  other arithmetic  15.2 us (5%)
  between operations  5.06 us (2%)
    ppermute x20, starting transfers between devices, passed_along(): lax.ppermute(value, axis, [(source, source + steps) for source in range(f...  113 us
    ppermute x20, waiting for transfers between devices, passed_along(): lax.ppermute(value, axis, [(source, source + steps) for source in range(f...  38.9 us
    all_gather x1, blocking collectives, local(): shards = lax.all_gather(gain_grads, ('dp', 'ctx'))  38.4 us
    unnamed x33, local copies, waits for them, and re-layouts  17.3 us
    dot_general x4, matrix products, attend(): mixture = jnp.einsum('hqk,khe->qhe', probability, shaped)  16.3 us
    ppermute x8, local copies, waits for them, and re-layouts, passed_along(): lax.ppermute(value, axis, [(source, source + steps) for source in range(f...  13.2 us
    dot_general x4, matrix products, attend(): jnp.einsum('qhe,khe->hqk', queries, key_vecs)  12.8 us
    another operation x1, other arithmetic  6.1 us
  transfers between devices with their start and end apart: 22, of which 9 were waited for; matrix products, arithmetic and copies ran while one was open for 31% of the time, Pallas kernels for 0%

profile of v1, /device:TPU:0, one launch (start us, length us, event | category | flops | bytes accessed | tf_op | source)
XLA Modules:
  0.0 287.3 jit_solution(7904127700236186597)
XLA Ops:
  0.6 6.0 %collective-permute-start.13 = (bf16[128,2048]{1,0:T(8,128)(2,1)}, bf16[128,2048]{1,0:T(8,128)(2,1)S(1)}, u32[]{:S(2)}, u32[]{:S(2)}) collective-permute-start(bf16[128,2048]{1,0:T(8,128)(2,1)} %bitcast.88), channel_id=1, source_target_pairs={{0,4},{1,5},{2,6},{3,7},{8,12},{9,13},{10,14},{11,15},{16,20},{17,... | collective-permute-start | bytes 1572872 | tf_op jit(solution)/shard_map/ppermute | solution.py:17
  6.6 4.5 %collective-permute-start.14 = (bf16[128,2048]{1,0:T(8,128)(2,1)}, bf16[128,2048]{1,0:T(8,128)(2,1)S(1)}, u32[]{:S(2)}, u32[]{:S(2)}) collective-permute-start(bf16[128,2048]{1,0:T(8,128)(2,1)} %bitcast.89), channel_id=1, source_target_pairs={{0,3},{1,4},{2,5},{3,6},{4,7},{8,11},{9,12},{10,13},{11,14},{12,15... | collective-permute-start | bytes 1572872 | tf_op jit(solution)/shard_map/ppermute | solution.py:17
  11.1 1.3 collective-permute-start.15
  12.4 3.9 %collective-permute-start.16 = (bf16[128,2048]{1,0:T(8,128)(2,1)}, bf16[128,2048]{1,0:T(8,128)(2,1)}, u32[]{:S(2)}, u32[]{:S(2)}) collective-permute-start(bf16[128,2048]{1,0:T(8,128)(2,1)} %bitcast.91), channel_id=1, source_target_pairs={{0,1},{1,2},{2,3},{3,4},{4,5},{5,6},{6,7},{8,9},{9,10},{10,11},{11... | collective-permute-start | bytes 1572872 | tf_op jit(solution)/shard_map/ppermute | solution.py:17
  17.6 1.3 fusion.62
  21.5 2.0 copy.64
  23.5 1.3 copy.59
  26.1 2.1 copy.55
  32.1 8.5 %collective-permute-done.4 = s32[128]{0:T(128)S(1)} collective-permute-done((s32[128]{0:T(128)}, s32[128]{0:T(128)S(1)}, u32[]{:S(2)}, u32[]{:S(2)}) %collective-permute-start.4) | collective-permute-done | bytes 544 | tf_op jit(solution)/shard_map/ppermute | solution.py:17
  40.6 38.0 %collective-permute-start.5 = (s32[128]{0:T(128)}, s32[128]{0:T(128)S(1)}, u32[]{:S(2)}, u32[]{:S(2)}) collective-permute-start(s32[128]{0:T(128)} %bitcast.119), channel_id=1, source_target_pairs={{0,3},{1,4},{2,5},{3,6},{4,7},{8,11},{9,12},{10,13},{11,14},{12,15... | collective-permute-start | bytes 1544 | tf_op jit(solution)/shard_map/ppermute | solution.py:17
  78.6 1.4 collective-permute-done.5
  81.3 1.4 collective-permute-done.6
  82.7 6.2 %collective-permute-start.7 = (s32[128]{0:T(128)}, s32[128]{0:T(128)S(1)}, u32[]{:S(2)}, u32[]{:S(2)}) collective-permute-start(s32[128]{0:T(128)} %bitcast.121), channel_id=1, source_target_pairs={{0,1},{1,2},{2,3},{3,4},{4,5},{5,6},{6,7},{8,9},{9,10},{10,11},{11... | collective-permute-start | bytes 1544 | tf_op jit(solution)/shard_map/ppermute | solution.py:17
  89.0 1.4 collective-permute-done.7
  90.4 6.8 %collective-permute-start.9 = (s32[128]{0:T(128)}, s32[128]{0:T(128)S(1)}, u32[]{:S(2)}, u32[]{:S(2)}) collective-permute-start(s32[128]{0:T(128)} %bitcast.113), channel_id=1, source_target_pairs={{0,4},{1,5},{2,6},{3,7},{8,12},{9,13},{10,14},{11,15},{16,20},{17,... | collective-permute-start | bytes 1544 | tf_op jit(solution)/shard_map/ppermute | solution.py:17
  98.6 4.1 %collective-permute-start.10 = (s32[128]{0:T(128)}, s32[128]{0:T(128)S(1)}, u32[]{:S(2)}, u32[]{:S(2)}) collective-permute-start(s32[128]{0:T(128)} %bitcast.114), channel_id=1, source_target_pairs={{0,3},{1,4},{2,5},{3,6},{4,7},{8,11},{9,12},{10,13},{11,14},{12,15... | collective-permute-start | bytes 1544 | tf_op jit(solution)/shard_map/ppermute | solution.py:17
  102.8 1.4 collective-permute-done.10
  104.2 3.4 %collective-permute-start.11 = (s32[128]{0:T(128)}, s32[128]{0:T(128)S(1)}, u32[]{:S(2)}, u32[]{:S(2)}) collective-permute-start(s32[128]{0:T(128)} %bitcast.115), channel_id=1, source_target_pairs={{0,2},{1,3},{2,4},{3,5},{4,6},{5,7},{8,10},{9,11},{10,12},{11,13},... | collective-permute-start | bytes 1544 | tf_op jit(solution)/shard_map/ppermute | solution.py:17
  107.6 1.4 collective-permute-done.11
  109.0 4.1 %collective-permute-start.12 = (s32[128]{0:T(128)}, s32[128]{0:T(128)S(1)}, u32[]{:S(2)}, u32[]{:S(2)}) collective-permute-start(s32[128]{0:T(128)} %bitcast.116), channel_id=1, source_target_pairs={{0,1},{1,2},{2,3},{3,4},{4,5},{5,6},{6,7},{8,9},{9,10},{10,11},{11... | collective-permute-start | bytes 1544 | tf_op jit(solution)/shard_map/ppermute | solution.py:17
  113.1 1.4 collective-permute-done.12
  114.5 19.6 %collective-permute-start = (bf16[128,2048]{1,0:T(8,128)(2,1)}, bf16[128,2048]{1,0:T(8,128)(2,1)}, u32[]{:S(2)}, u32[]{:S(2)}) collective-permute-start(bf16[128,2048]{1,0:T(8,128)(2,1)} %bitcast), channel_id=1, source_target_pairs={{0,4},{1,5},{2,6},{3,7},{8,12},{9,13},{10,14},{11,15},{16,20},{17,... | collective-permute-start | bytes 1572872 | tf_op jit(solution)/shard_map/ppermute | solution.py:17
  135.8 2.1 collective-permute-start.1
  138.9 2.1 collective-permute-start.2
  142.0 3.3 %collective-permute-start.3 = (bf16[128,2048]{1,0:T(8,128)(2,1)}, bf16[128,2048]{1,0:T(8,128)(2,1)}, u32[]{:S(2)}, u32[]{:S(2)}) collective-permute-start(bf16[128,2048]{1,0:T(8,128)(2,1)} %bitcast), channel_id=1, source_target_pairs={{0,1},{1,2},{2,3},{3,4},{4,5},{5,6},{6,7},{8,9},{9,10},{10,11},{11... | collective-permute-start | bytes 1572872 | tf_op jit(solution)/shard_map/ppermute | solution.py:17
  149.9 2.0 copy.63
  156.0 2.7 fusion.14
  158.8 4.1 %fusion.59 = (bf16[16,128,640]{2,1,0:T(8,128)(2,1)}, f32[16,128]{1,0:T(8,128)S(1)}, f32[16,128,640]{2,1,0:T(8,128)S(1)}) fusion(f32[16,128]{1,0:T(8,128)S(1)} %get-tuple-element.51, f32[16,128,640]{2,1,0:T(8,128)S(1)} %get-tuple-element.52, pred[128,640]{1,0:T(8,128)(4,1)S(1)} %get-tuple-element.45, f32[16,128]{1,0:T(8,128)S(1)} %multiply_divide_fusion, ...), kind=kOutput, calls=%fused_computation.121 | convolution fusion | flops 345241600 | bytes 16367616 | tf_op jit(solution)/shard_map/transpose(jvp(hqk,khe->qhe))/dot_general | solution.py:53
  162.9 3.4 %multiply_reduce_fusion.1 = (f32[16,128]{1,0:T(8,128)S(1)}, f32[128,16,128]{0,2,1:T(8,128)S(1)}) fusion(f32[640,16,128]{0,2,1:T(8,128)S(1)} %get-tuple-element.29, f32[16,128]{1,0:T(8,128)S(1)} %bitcast.106, bf16[640,16,128]{0,2,1:T(8,128)(2,1)S(1)} %get-tuple-element.30, bf16[640,16,128]{0,2,1:T(8,128)(2,1)S(1)} %constant_dynamic-update-slice_fusion.7, ...), kind=kOutput, calls=%fused_computation.58 | convolution fusion | flops 352057344 | bytes 17989632 | tf_op jit(solution)/shard_map/transpose(jvp(qhe,khe->hqk))/dot_general | solution.py:40
  166.3 3.9 %fusion.6 = (f32[16,128]{1,0:T(8,128)S(1)}, f32[640,16]{0,1:T(8,128)S(1)}, f32[16,640,128]{1,2,0:T(8,128)S(1)}) fusion(bf16[640,16,128]{0,2,1:T(8,128)(2,1)S(1)} %constant_dynamic-update-slice_fusion.7, f32[640,16]{0,1:T(8,128)S(1)} %fusion.54, f32[128,16,128]{0,2,1:T(8,128)S(1)} %get-tuple-element.38, f32[16,128]{1,0:T(8,128)S(1)} %bitcast.102, ...), kind=kOutput, calls=%fused_computation.19 | convolution fusion | flops 354930688 | bytes 21176320 | tf_op jit(solution)/shard_map/transpose(jvp(qhe,khe->hqk))/dot_general | solution.py:40
  170.3 4.0 %fusion.27 = f32[16,128]{1,0:T(8,128)S(1)} fusion(f32[128,16,128]{2,0,1:T(8,128)S(1)} %copy-done.2, bf16[640,16,128]{0,2,1:T(8,128)(2,1)S(1)} %constant_dynamic-update-slice_fusion.7, bf16[16,128,640]{2,1,0:T(8,128)(2,1)} %get-tuple-element.27, f32[16,128,640]{2,1,0:T(8,128)S(1)} %get-tuple-element.52, f32[16,128]{1,0:T(8,128)S(1)} %get-tuple-element.51, ...), kind=kOutput, calls=%fused_computation.50 | convolution fusion | flops 343930880 | bytes 11632640 | tf_op jit(solution)/shard_map/jvp(hqk,khe->qhe)/dot_general | solution.py:53
  174.3 4.9 %add_add_fusion = f32[640,16,128]{0,2,1:T(8,128)} fusion(bf16[640,16,128]{0,2,1:T(8,128)(2,1)S(1)} %constant_dynamic-update-slice_fusion.7, f32[128,16,128]{0,2,1:T(8,128)S(1)} %get-tuple-element.38, f32[16,640,128]{1,2,0:T(8,128)S(1)} %get-tuple-element.54, f32[640,16]{0,1:T(8,128)S(1)} %multiply_multiply_fusion.1, f32[16,128]{1,0:T(8,128)S(1)} %bitcast.103, ...), kind=kOutput, calls=%fused_computation.4 | convolution fusion | flops 354418688 | bytes 22732800 | tf_op jit(solution)/shard_map/transpose(jvp(hqk,khe->qhe))/dot_general | solution.py:53
  179.2 6.0 %copy.69 = f32[640,2048]{1,0:T(8,128)} copy(f32[640,2048]{0,1:T(8,128)} %bitcast.72) | data formatting | bytes 10485760 | tf_op jit(solution)/shard_map/transpose(jvp())/reshape | solution.py:34
  185.1 6.1 %fusion.60 = (bf16[640,2048]{1,0:T(8,128)(2,1)S(1)}, f32[640,2048]{1,0:T(8,128)}) fusion(f32[640,2048]{1,0:T(8,128)} %copy.69, bf16[128,2048]{1,0:T(8,128)(2,1)S(1)} %bitcast.86), kind=kLoop, calls=%fused_computation.122 | loop fusion | flops 3932160 | bytes 13631488 | tf_op jit(solution)/shard_map/convert.8
  191.2 1.4 fusion.61
  192.6 1.4 collective-permute-start.17
  194.1 1.3 collective-permute-start.18
  195.4 2.0 copy.51
  197.4 1.5 collective-permute-start.19
  198.9 2.0 copy.52
  202.2 2.0 copy.53
  207.8 2.0 copy.54
  212.9 2.8 fusion.12
  216.8 3.3 %fusion.2 = f32[16,128,128]{2,1,0:T(8,128)} fusion(bf16[640,16,128]{0,2,1:T(8,128)(2,1)S(1)} %constant_dynamic-update-slice_fusion, bf16[16,128,640]{2,1,0:T(8,128)(2,1)S(1)} %fusion.29, f32[16,128,640]{2,1,0:T(8,128)S(1)} %get-tuple-element.50, f32[16,128]{1,0:T(8,128)S(1)} %get-tuple-element.49, pred[128,640]{1,0:T(8,128)(4,1)S(1)} %get-tuple-element.46), kind=kOutput, calls=%fused_computation.13 | convolution fusion | flops 343408640 | bytes 11624448 | tf_op jit(solution)/shard_map/hqk,khe->qhe/dot_general | solution.py:53
  220.1 1.6 copy.58
  223.0 21.2 %collective-permute-done.20 = bf16[128,2048]{1,0:T(8,128)(2,1)} collective-permute-done((bf16[128,2048]{1,0:T(8,128)(2,1)}, bf16[128,2048]{1,0:T(8,128)(2,1)}, u32[]{:S(2)}, u32[]{:S(2)}) %collective-permute-start.20) | collective-permute-done | bytes 524320 | tf_op jit(solution)/shard_map/ppermute | solution.py:17
  244.3 2.2 fusion.30
  246.5 38.4 %all-gather.1 = f32[16,3,2048]{2,1,0:T(4,128)S(1)} all-gather(f32[1,3,2048]{2,1,0:T(4,128)S(1)} %add_bitcast_fusion), channel_id=2, replica_groups=mesh['dp'=2,'pipe'=2,'ctx'=8] {'dp','ctx'}, dimensions={0}, use_global_device_ids=true | all-gather | bytes 417792 | tf_op jit(solution)/shard_map/all_gather | solution.py:119
  (87 shorter events, 32.8 us)
Async XLA Ops:
  0.6 135.2 %collective-permute-start.13 = (bf16[128,2048]{1,0:T(8,128)(2,1)}, bf16[128,2048]{1,0:T(8,128)(2,1)S(1)}, u32[]{:S(2)}, u32[]{:S(2)}) collective-permute-start(bf16[128,2048]{1,0:T(8,128)(2,1)} %bitcast.88), channel_id=1, source_target_pairs={{0,4},{1,5},{2,6},{3,7},{8,12},{9,13},{10,14},{11,15},{16,20},{17,... | collective-permute-start | bytes 1572872 | tf_op jit(solution)/shard_map/ppermute | solution.py:17
  6.6 132.3 %collective-permute-start.14 = (bf16[128,2048]{1,0:T(8,128)(2,1)}, bf16[128,2048]{1,0:T(8,128)(2,1)S(1)}, u32[]{:S(2)}, u32[]{:S(2)}) collective-permute-start(bf16[128,2048]{1,0:T(8,128)(2,1)} %bitcast.89), channel_id=1, source_target_pairs={{0,3},{1,4},{2,5},{3,6},{4,7},{8,11},{9,12},{10,13},{11,14},{12,15... | collective-permute-start | bytes 1572872 | tf_op jit(solution)/shard_map/ppermute | solution.py:17
  11.1 130.9 %collective-permute-start.15 = (bf16[128,2048]{1,0:T(8,128)(2,1)}, bf16[128,2048]{1,0:T(8,128)(2,1)S(1)}, u32[]{:S(2)}, u32[]{:S(2)}) collective-permute-start(bf16[128,2048]{1,0:T(8,128)(2,1)} %bitcast.90), channel_id=1, source_target_pairs={{0,2},{1,3},{2,4},{3,5},{4,6},{5,7},{8,10},{9,11},{10,12},{11,13},... | collective-permute-start | bytes 1572872 | tf_op jit(solution)/shard_map/ppermute | solution.py:17
  12.4 137.4 %collective-permute-start.16 = (bf16[128,2048]{1,0:T(8,128)(2,1)}, bf16[128,2048]{1,0:T(8,128)(2,1)}, u32[]{:S(2)}, u32[]{:S(2)}) collective-permute-start(bf16[128,2048]{1,0:T(8,128)(2,1)} %bitcast.91), channel_id=1, source_target_pairs={{0,1},{1,2},{2,3},{3,4},{4,5},{5,6},{6,7},{8,9},{9,10},{10,11},{11... | collective-permute-start | bytes 1572872 | tf_op jit(solution)/shard_map/ppermute | solution.py:17
  16.3 24.3 %collective-permute-start.4 = (s32[128]{0:T(128)}, s32[128]{0:T(128)S(1)}, u32[]{:S(2)}, u32[]{:S(2)}) collective-permute-start(s32[128]{0:T(128)} %bitcast.118), channel_id=1, source_target_pairs={{0,4},{1,5},{2,6},{3,7},{8,12},{9,13},{10,14},{11,15},{16,20},{17,... | collective-permute-start | bytes 1544 | tf_op jit(solution)/shard_map/ppermute | solution.py:17
  40.6 39.4 %collective-permute-start.5 = (s32[128]{0:T(128)}, s32[128]{0:T(128)S(1)}, u32[]{:S(2)}, u32[]{:S(2)}) collective-permute-start(s32[128]{0:T(128)} %bitcast.119), channel_id=1, source_target_pairs={{0,3},{1,4},{2,5},{3,6},{4,7},{8,11},{9,12},{10,13},{11,14},{12,15... | collective-permute-start | bytes 1544 | tf_op jit(solution)/shard_map/ppermute | solution.py:17
  80.0 2.7 collective-permute-start.6
  82.7 7.6 %collective-permute-start.7 = (s32[128]{0:T(128)}, s32[128]{0:T(128)S(1)}, u32[]{:S(2)}, u32[]{:S(2)}) collective-permute-start(s32[128]{0:T(128)} %bitcast.121), channel_id=1, source_target_pairs={{0,1},{1,2},{2,3},{3,4},{4,5},{5,6},{6,7},{8,9},{9,10},{10,11},{11... | collective-permute-start | bytes 1544 | tf_op jit(solution)/shard_map/ppermute | solution.py:17
  90.4 8.2 %collective-permute-start.9 = (s32[128]{0:T(128)}, s32[128]{0:T(128)S(1)}, u32[]{:S(2)}, u32[]{:S(2)}) collective-permute-start(s32[128]{0:T(128)} %bitcast.113), channel_id=1, source_target_pairs={{0,4},{1,5},{2,6},{3,7},{8,12},{9,13},{10,14},{11,15},{16,20},{17,... | collective-permute-start | bytes 1544 | tf_op jit(solution)/shard_map/ppermute | solution.py:17
  98.6 5.6 %collective-permute-start.10 = (s32[128]{0:T(128)}, s32[128]{0:T(128)S(1)}, u32[]{:S(2)}, u32[]{:S(2)}) collective-permute-start(s32[128]{0:T(128)} %bitcast.114), channel_id=1, source_target_pairs={{0,3},{1,4},{2,5},{3,6},{4,7},{8,11},{9,12},{10,13},{11,14},{12,15... | collective-permute-start | bytes 1544 | tf_op jit(solution)/shard_map/ppermute | solution.py:17
  104.2 4.8 %collective-permute-start.11 = (s32[128]{0:T(128)}, s32[128]{0:T(128)S(1)}, u32[]{:S(2)}, u32[]{:S(2)}) collective-permute-start(s32[128]{0:T(128)} %bitcast.115), channel_id=1, source_target_pairs={{0,2},{1,3},{2,4},{3,5},{4,6},{5,7},{8,10},{9,11},{10,12},{11,13},... | collective-permute-start | bytes 1544 | tf_op jit(solution)/shard_map/ppermute | solution.py:17
  109.0 5.6 %collective-permute-start.12 = (s32[128]{0:T(128)}, s32[128]{0:T(128)S(1)}, u32[]{:S(2)}, u32[]{:S(2)}) collective-permute-start(s32[128]{0:T(128)} %bitcast.116), channel_id=1, source_target_pairs={{0,1},{1,2},{2,3},{3,4},{4,5},{5,6},{6,7},{8,9},{9,10},{10,11},{11... | collective-permute-start | bytes 1544 | tf_op jit(solution)/shard_map/ppermute | solution.py:17
  114.5 79.5 %collective-permute-start = (bf16[128,2048]{1,0:T(8,128)(2,1)}, bf16[128,2048]{1,0:T(8,128)(2,1)}, u32[]{:S(2)}, u32[]{:S(2)}) collective-permute-start(bf16[128,2048]{1,0:T(8,128)(2,1)} %bitcast), channel_id=1, source_target_pairs={{0,4},{1,5},{2,6},{3,7},{8,12},{9,13},{10,14},{11,15},{16,20},{17,... | collective-permute-start | bytes 1572872 | tf_op jit(solution)/shard_map/ppermute | solution.py:17
  135.8 61.6 %collective-permute-start.1 = (bf16[128,2048]{1,0:T(8,128)(2,1)}, bf16[128,2048]{1,0:T(8,128)(2,1)}, u32[]{:S(2)}, u32[]{:S(2)}) collective-permute-start(bf16[128,2048]{1,0:T(8,128)(2,1)} %bitcast), channel_id=1, source_target_pairs={{0,3},{1,4},{2,5},{3,6},{4,7},{8,11},{9,12},{10,13},{11,14},{12,15... | collective-permute-start | bytes 1572872 | tf_op jit(solution)/shard_map/ppermute | solution.py:17
  138.9 62.1 %collective-permute-start.2 = (bf16[128,2048]{1,0:T(8,128)(2,1)}, bf16[128,2048]{1,0:T(8,128)(2,1)}, u32[]{:S(2)}, u32[]{:S(2)}) collective-permute-start(bf16[128,2048]{1,0:T(8,128)(2,1)} %bitcast), channel_id=1, source_target_pairs={{0,2},{1,3},{2,4},{3,5},{4,6},{5,7},{8,10},{9,11},{10,12},{11,13},... | collective-permute-start | bytes 1572872 | tf_op jit(solution)/shard_map/ppermute | solution.py:17
  142.0 65.8 %collective-permute-start.3 = (bf16[128,2048]{1,0:T(8,128)(2,1)}, bf16[128,2048]{1,0:T(8,128)(2,1)}, u32[]{:S(2)}, u32[]{:S(2)}) collective-permute-start(bf16[128,2048]{1,0:T(8,128)(2,1)} %bitcast), channel_id=1, source_target_pairs={{0,1},{1,2},{2,3},{3,4},{4,5},{5,6},{6,7},{8,9},{9,10},{10,11},{11... | collective-permute-start | bytes 1572872 | tf_op jit(solution)/shard_map/ppermute | solution.py:17
  166.3 3.9 %copy-start.2 = (f32[128,16,128]{2,0,1:T(8,128)S(1)}, f32[128,16,128]{2,0,1:T(8,128)}, u32[]{:S(2)}) copy-start(f32[128,16,128]{2,0,1:T(8,128)} %copy.71) | copy-start | bytes 3145732
  170.3 4.0 %copy-start.3 = (bf16[16,128,640]{2,1,0:T(8,128)(2,1)S(1)}, bf16[16,128,640]{2,1,0:T(8,128)(2,1)}, u32[]{:S(2)}) copy-start(bf16[16,128,640]{2,1,0:T(8,128)(2,1)} %get-tuple-element.27) | copy-start | bytes 7864324
  179.2 6.0 %copy-start.1 = (bf16[1,1,128,2048]{3,2,1,0:T(8,128)(2,1)S(1)}, bf16[1,1,128,2048]{3,2,1,0:T(8,128)(2,1)}, u32[]{:S(2)}) copy-start(bf16[1,1,128,2048]{3,2,1,0:T(8,128)(2,1)} %param.16) | copy-start | bytes 1572868
  192.6 18.4 %copy-start = (bf16[1,1,128,2048]{2,3,1,0:T(8,128)(2,1)S(1)}, bf16[1,1,128,2048]{2,3,1,0:T(8,128)(2,1)}, u32[]{:S(2)}) copy-start(bf16[1,1,128,2048]{2,3,1,0:T(8,128)(2,1)} %copy.55) | copy-start | bytes 1572868
  192.6 30.4 %collective-permute-start.17 = (bf16[128,2048]{1,0:T(8,128)(2,1)}, bf16[128,2048]{1,0:T(8,128)(2,1)}, u32[]{:S(2)}, u32[]{:S(2)}) collective-permute-start(bf16[128,2048]{1,0:T(8,128)(2,1)} %get-tuple-element.33), channel_id=1, source_target_pairs={{1,0},{2,1},{3,2},{4,3},{5,4},{6,5},{7,6},{9,8},{10,9},{11,10},{12... | collective-permute-start | bytes 1572872 | tf_op jit(solution)/shard_map/ppermute | solution.py:17
  194.1 28.9 %collective-permute-start.18 = (bf16[128,2048]{1,0:T(8,128)(2,1)}, bf16[128,2048]{1,0:T(8,128)(2,1)}, u32[]{:S(2)}, u32[]{:S(2)}) collective-permute-start(bf16[128,2048]{1,0:T(8,128)(2,1)} %get-tuple-element.36), channel_id=1, source_target_pairs={{2,0},{3,1},{4,2},{5,3},{6,4},{7,5},{10,8},{11,9},{12,10},{13,11},... | collective-permute-start | bytes 1572872 | tf_op jit(solution)/shard_map/ppermute | solution.py:17
  197.4 25.6 %collective-permute-start.19 = (bf16[128,2048]{1,0:T(8,128)(2,1)}, bf16[128,2048]{1,0:T(8,128)(2,1)}, u32[]{:S(2)}, u32[]{:S(2)}) collective-permute-start(bf16[128,2048]{1,0:T(8,128)(2,1)} %get-tuple-element.35), channel_id=1, source_target_pairs={{3,0},{4,1},{5,2},{6,3},{7,4},{11,8},{12,9},{13,10},{14,11},{15,12... | collective-permute-start | bytes 1572872 | tf_op jit(solution)/shard_map/ppermute | solution.py:17
  201.0 43.3 %collective-permute-start.20 = (bf16[128,2048]{1,0:T(8,128)(2,1)}, bf16[128,2048]{1,0:T(8,128)(2,1)}, u32[]{:S(2)}, u32[]{:S(2)}) collective-permute-start(bf16[128,2048]{1,0:T(8,128)(2,1)} %get-tuple-element.34), channel_id=1, source_target_pairs={{4,0},{5,1},{6,2},{7,3},{12,8},{13,9},{14,10},{15,11},{20,16},{21,... | collective-permute-start | bytes 1572872 | tf_op jit(solution)/shard_map/ppermute | solution.py:17
  222.9 62.8 %collective-permute-start.8 = (bf16[128,2048]{1,0:T(8,128)(2,1)S(1)}, bf16[128,2048]{1,0:T(8,128)(2,1)S(1)}, u32[]{:S(2)}, u32[]{:S(2)}) collective-permute-start(bf16[128,2048]{1,0:T(8,128)(2,1)S(1)} %add_convert_fusion), channel_id=1, source_target_pairs={{0,8},{8,0},{1,9},{9,1},{2,10},{10,2},{3,11},{11,3},{4,12},{12,4},... | collective-permute-start | bytes 1572872 | tf_op jit(solution)/shard_map/ppermute | solution.py:23
  246.5 39.2 %collective-permute-start.21 = (bf16[128,2048]{1,0:T(8,128)(2,1)S(1)}, bf16[128,2048]{1,0:T(8,128)(2,1)S(1)}, u32[]{:S(2)}, u32[]{:S(2)}) collective-permute-start(bf16[128,2048]{1,0:T(8,128)(2,1)S(1)} %fusion.30), channel_id=1, source_target_pairs={{0,8},{8,0},{1,9},{9,1},{2,10},{10,2},{3,11},{11,3},{4,12},{12,4},... | collective-permute-start | bytes 1572872 | tf_op jit(solution)/shard_map/ppermute | solution.py:23
